TPU v7x, 32 devices: a whole 2x2x4 slice. The times are simulated.
32 devices in a mesh: group: 2 (over y), lat: 4 (over z), chan: 2 (over x), lon: 2 (over core).
Axes of the slice: x: 2, y: 2, z: 4, core: 2. Of those that a mesh axis runs over, the one named last changes fastest.
Arguments:
- features: bfloat16 [32, 1440, 640], P('group', ('chan', 'lon'), 'lat'), parts along dimension 0, may hold values from -6 to 6
- basis: bfloat16 [16, 2, 5, 5], replicated, may hold values from -1.25 to 1.25
- block_start: int32 [16], replicated, may hold values from 0 to 4, as said below
- block_width: int32 [16], replicated, may hold values from 1 to 5, as said below
- weight: bfloat16 [1280, 640], P(None, ('chan', 'lon')), may hold values from -0.15625 to 0.15625
- cotangent: bfloat16 [32, 1440, 640], P(('group', 'lat'), ('chan', 'lon')), parts along dimension 0, may hold values from -6 to 6
Outputs:
- output: bfloat16 [32, 1440, 640], P(('group', 'lat'), ('chan', 'lon')), parts along dimension 0
- grad_input: bfloat16 [32, 1440, 640], P(('group', 'lat'), ('chan', 'lon')), parts along dimension 0
- grad_weight: float32 [2560, 640], P(('group', 'lat', 'chan', 'lon')), parts along dimension 0
There are 2 independent parts, one for each index of `group`. A program takes and returns all parts, laid end to end along the dimension named above; an argument that names none is the same for every part. Nothing has to cross between parts.
Inputs may be any that keep to these rules, and one draw needn't show every extreme that they name: block_start + block_width <= 5 for every row; some row has block_start 5 - 1. Some row has block_width 5 and some row block_width 1.
All inputs are finite; a program needn't handle non-finite values.
Results may differ from a plain program's by a relative error of at most 0.005.
Values may be sent and summed in bfloat16 or wider, within the bound.
A program may use at most 128 MiB of HBM per device.

v0:
```python
import functools
import math

import jax
import jax.numpy as jnp
from jax import lax
from jax.experimental import pallas as pl
from jax.experimental.pallas import tpu as pltpu
from jax.sharding import PartitionSpec as P

REACH = 2


def padded(array, sides, width):
    for axis, dim in sides:
        size, length = (lax.axis_size(axis), array.shape[dim])
        up = [(i, (i + 1) % size) for i in range(size)]
        down = [(j, i) for i, j in up]
        last = lax.slice_in_dim(array, length - width, length, axis=dim)
        initial = lax.slice_in_dim(array, 0, width, axis=dim)
        before = lax.ppermute(last, axis, up)
        after = lax.ppermute(initial, axis, down)
        array = jnp.concatenate([before, array, after], axis=dim)
    return array


def extend(field, first, total_rows):
    haloed = padded(field, (("lat", 0), (("chan", "lon"), 1)), REACH)
    position = first - REACH + jnp.arange(haloed.shape[0], dtype=jnp.int32)
    inside = (position >= 0) & (position < total_rows)
    return jnp.where(inside[:, None, None], haloed, jnp.zeros_like(haloed))


def plain(features, basis, block_start, block_width, weight, cotangent):
    local = lax.all_to_all(features, "lat", split_axis=0, concat_axis=2, tiled=True)
    rows, width, chans = local.shape
    nbasis = basis.shape[1]
    span = 2 * REACH + 1
    total_rows = rows * lax.axis_size("lat")
    first = lax.axis_index("lat") * rows
    column = jnp.arange(span, dtype=jnp.int32)
    valid = (column[None, :] >= block_start[:, None]) & (
        column[None, :] < (block_start + block_width)[:, None]
    )
    blocks = jnp.where(valid[:, None, None, :], basis, jnp.zeros_like(basis))
    padded_blocks = jnp.pad(blocks, ((REACH, REACH), (0, 0), (0, 0), (0, 0)))
    near_blocks = lax.dynamic_slice_in_dim(padded_blocks, first, rows + 2 * REACH, 0).astype(
        jnp.float32
    )
    own_blocks = near_blocks[REACH : REACH + rows]
    reach_cols = width + 2 * REACH
    shift_table = (
        jnp.arange(reach_cols, dtype=jnp.int32)[None, :, None]
        - jnp.arange(width, dtype=jnp.int32)[:, None, None]
        == column[None, None, :]
    ).astype(jnp.float32)
    back_table = shift_table[:, :, ::-1]
    haloed = extend(local, first, total_rows)
    feat_parts = []
    for basis_k in range(nbasis):
        running = jnp.zeros((rows, width, chans), jnp.float32)
        for offset in range(span):
            row_map = jnp.einsum(
                "lmb,ib->ilm", shift_table, own_blocks[:, basis_k, offset, :]
            ).astype(jnp.bfloat16)
            running = running + jnp.einsum(
                "ilm,imc->ilc",
                row_map,
                haloed[offset : offset + rows],
                preferred_element_type=jnp.float32,
            )
        feat_parts.append(running.astype(jnp.bfloat16))
    feats = jnp.concatenate(feat_parts, axis=2)
    mixed = jnp.einsum(
        "ilj,jo->ilo",
        feats,
        lax.all_gather(weight, ("chan", "lon"), axis=1, tiled=True),
        preferred_element_type=jnp.float32,
    )
    grad_feats = jnp.einsum(
        "ilo,jo->ilj",
        cotangent,
        lax.all_gather(weight, ("chan", "lon"), axis=1, tiled=True),
        preferred_element_type=jnp.float32,
    )
    output = mixed.astype(jnp.bfloat16)
    factor = 1.0 / math.sqrt(total_rows * width * lax.axis_size(("chan", "lon")))
    grad_weight = lax.psum_scatter(
        lax.dot_general(
            feats, cotangent, (((0, 1), (0, 1)), ((), ())), preferred_element_type=jnp.float32
        )
        * factor,
        ("lat", "chan", "lon"),
        scatter_dimension=0,
        tiled=True,
    )
    grad_feats = grad_feats.astype(jnp.bfloat16)
    grad_halo = extend(grad_feats, first, total_rows)
    result = jnp.zeros((rows, width, chans), jnp.float32)
    for offset in range(span):
        begin = 2 * REACH - offset
        source_rows = grad_halo[begin : begin + rows]
        block_rows = near_blocks[begin : begin + rows]
        for basis_k in range(nbasis):
            back_map = jnp.einsum(
                "nmb,jb->jnm", back_table, block_rows[:, basis_k, offset, :]
            ).astype(jnp.bfloat16)
            source_part = source_rows[:, :, basis_k * chans : (basis_k + 1) * chans]
            result = result + jnp.einsum(
                "jnm,jmc->jnc", back_map, source_part, preferred_element_type=jnp.float32
            )
    grad_input = result.astype(jnp.bfloat16)
    return (output, grad_input, grad_weight)


SPAN = 2 * REACH + 1
TILE = 128
WINDOW = TILE + 16
MESH = pl.DeviceIdType.MESH


def ring_edges(array):
    axes = ("chan", "lon")
    size, width = lax.axis_size(axes), array.shape[1]
    up = [(i, (i + 1) % size) for i in range(size)]
    before = lax.ppermute(array[:, width - REACH :], axes, up)
    after = lax.ppermute(array[:, :REACH], axes, [(j, i) for i, j in up])
    fill = -(width + 2 * REACH) % 16
    zeros = jnp.zeros((array.shape[0], fill, array.shape[2]), array.dtype)
    return jnp.concatenate([before, array, after, zeros], axis=1)


def band_maps(basis, block_start, block_width, rows):
    column = jnp.arange(SPAN, dtype=jnp.int32)
    valid = (column[None, :] >= block_start[:, None]) & (
        column[None, :] < (block_start + block_width)[:, None]
    )
    blocks = jnp.where(valid[:, None, None, :], basis, jnp.zeros_like(basis))
    blocks = jnp.pad(blocks, ((REACH, REACH), (0, 0), (0, 0), (0, 0)))
    first = lax.axis_index("lat") * rows
    near = lax.dynamic_slice_in_dim(blocks, first, rows + 2 * REACH, 0)
    own = near[REACH : REACH + rows]
    nbasis = basis.shape[1]
    shift = jnp.arange(WINDOW, dtype=jnp.int32)[None, :] - jnp.arange(TILE, dtype=jnp.int32)[:, None]
    forward = jnp.zeros((rows, nbasis, TILE, SPAN, WINDOW), basis.dtype)
    for b in range(SPAN):
        hit = (shift == b)[None, None, :, None, :]
        forward = jnp.where(hit, own[:, :, :, b][:, :, None, :, None], forward)
    source = jnp.stack(
        [jnp.stack([near[i + q, :, SPAN - 1 - q, :] for q in range(SPAN)]) for i in range(rows)]
    )
    backward = jnp.zeros((rows, TILE, SPAN, nbasis, WINDOW), basis.dtype)
    for b in range(SPAN):
        hit = (shift == SPAN - 1 - b)[None, :, None, None, :]
        backward = jnp.where(hit, source[:, None, :, :, b, None], backward)
    return (
        forward.reshape(rows, nbasis * TILE, SPAN * WINDOW),
        backward.reshape(rows, TILE, SPAN * nbasis * WINDOW),
    )


def layer_kernel(
    nlat, nchan, nlon, factor,
    field, cot_ext, weight_t, cot, forward, backward,
    out, grad_in, grad_w,
    landed, near, cots, mixing, gathered, feats, grads, total,
    send1, recv1, send2, recv2, send3, recv3,
    f_send, f_recv, fwd_send, w_send, w_recv, c_send, c_recv, own_sem, g_send, g_recv,
):
    z, x, core = lax.axis_index("lat"), lax.axis_index("chan"), lax.axis_index("lon")
    rows, width, chs = cot.shape
    ext, part = field.shape[1], field.shape[2]
    wide = near.shape[1]
    tiles = (width + TILE - 1) // TILE
    nshard = nchan * nlon
    mine = x * nlon + core
    block = grad_w.shape[0]
    last = rows + REACH

    barrier = pltpu.get_barrier_semaphore()
    for t in range(nlat):
        @pl.when(z != t)
        def _():
            pl.semaphore_signal(barrier, inc=1, device_id={"lat": t}, device_id_type=MESH)
    for s in range(nshard):
        @pl.when(mine != s)
        def _():
            pl.semaphore_signal(
                barrier, inc=1, device_id={"chan": s // nlon, "lon": s % nlon}, device_id_type=MESH
            )
    pl.semaphore_wait(barrier, nlat - 1 + nshard - 1)

    def piece(t, kind):
        if kind == 0:
            return rows * t, REACH, rows
        if kind == 1:
            return rows * t - REACH, 0, REACH
        return rows * (t + 1), last, REACH

    def field_copy(t, kind):
        begin, at, count = piece(t, kind)
        return pltpu.make_async_remote_copy(
            src_ref=field.at[pl.ds(begin, count)],
            dst_ref=landed.at[z, pl.ds(at, count)],
            send_sem=f_send.at[t, kind],
            recv_sem=f_recv.at[z, kind],
            device_id={"lat": t},
            device_id_type=MESH,
        )

    def arrival(j, kind):
        _, at, count = piece(1, kind)
        return pltpu.make_async_remote_copy(
            src_ref=field.at[pl.ds(0, count)],
            dst_ref=landed.at[j, pl.ds(at, count)],
            send_sem=f_send.at[0, kind],
            recv_sem=f_recv.at[j, kind],
            device_id={"lat": 0},
            device_id_type=MESH,
        )

    def direct(t, kind):
        if kind == 0:
            return z != t
        if kind == 1:
            return ((z > t) | (z == t - 1)) if t > 0 else None
        return ((z < t) | (z == t + 1)) if t < nlat - 1 else None

    kinds = ((t, kind) for kind in (0, 1, 2) for t in range(nlat))
    sends = [(t, kind, direct(t, kind)) for t, kind in kinds if direct(t, kind) is not None]
    for t, kind, when in sends:
        @pl.when(when)
        def _():
            field_copy(t, kind).start()

    def own_copy(t, kind):
        begin, at, count = piece(t, kind)
        return pltpu.make_async_copy(
            field.at[pl.ds(begin, count)], landed.at[t, pl.ds(at, count)], own_sem.at[kind]
        )

    for t, kind, _when in sends:
        @pl.when(z == t)
        def _():
            own_copy(t, kind).start()

    def weight_copy(s):
        return pltpu.make_async_remote_copy(
            src_ref=weight_t,
            dst_ref=gathered.at[mine],
            send_sem=w_send.at[s],
            recv_sem=w_recv.at[mine],
            device_id={"chan": s // nlon, "lon": s % nlon},
            device_id_type=MESH,
        )

    for s in range(nshard):
        @pl.when(mine != s)
        def _():
            weight_copy(s).start()
    own_weight = pltpu.make_async_copy(weight_t, gathered.at[mine], own_sem.at[3])
    own_weight.start()
    own_cot = pltpu.make_async_copy(cot_ext, cots.at[pl.ds(REACH, rows)], own_sem.at[4])
    own_cot.start()

    def cot_copy(way):
        begin, at = ((rows - REACH, 0), (0, last))[way]
        return pltpu.make_async_remote_copy(
            src_ref=cot_ext.at[pl.ds(begin, REACH)],
            dst_ref=cots.at[pl.ds(at, REACH)],
            send_sem=c_send.at[way],
            recv_sem=c_recv.at[way],
            device_id={"lat": z + 1 - 2 * way},
            device_id_type=MESH,
        )

    has_up, has_down = z < nlat - 1, z > 0

    @pl.when(has_up)
    def _():
        cot_copy(0).start()

    @pl.when(has_down)
    def _():
        cot_copy(1).start()

    if wide > ext:
        near[:, pl.ds(ext, wide - ext), :] = jnp.zeros((rows + 2 * REACH, wide - ext, chs), near.dtype)
        grads[:, pl.ds(ext, wide - ext), :] = jnp.zeros(
            (rows + 2 * REACH, wide - ext, grads.shape[2]), grads.dtype
        )

    @pl.when(jnp.logical_not(has_down))
    def _():
        cots[pl.ds(0, REACH)] = jnp.zeros((REACH, ext, chs), cots.dtype)
        landed[:, pl.ds(0, REACH)] = jnp.zeros((nlat, REACH, ext, part), landed.dtype)

    @pl.when(jnp.logical_not(has_up))
    def _():
        cots[pl.ds(last, REACH)] = jnp.zeros((REACH, ext, chs), cots.dtype)
        landed[:, pl.ds(last, REACH)] = jnp.zeros((nlat, REACH, ext, part), landed.dtype)

    own_weight.wait()
    for s in range(nshard):
        @pl.when(mine != s)
        def _():
            pltpu.make_async_remote_copy(
                src_ref=weight_t, dst_ref=gathered.at[s], send_sem=w_send.at[s],
                recv_sem=w_recv.at[s], device_id={"chan": s // nlon, "lon": s % nlon},
                device_id_type=MESH,
            ).wait_recv()
    mixing[...] = gathered[...].reshape(mixing.shape)

    def feature_gradient(q):
        grads[q, pl.ds(0, ext), :] = jnp.dot(
            cots[q], mixing[...], preferred_element_type=jnp.float32
        ).astype(grads.dtype)

    own_cot.wait()

    @pl.loop(REACH, last)
    def _(q):
        feature_gradient(q)

    def pass_on(j, way):
        begin, at, kind = ((last - REACH, 0, 1), (REACH, last, 2))[way]
        return pltpu.make_async_remote_copy(
            src_ref=landed.at[j, pl.ds(begin, REACH)],
            dst_ref=landed.at[j, pl.ds(at, REACH)],
            send_sem=fwd_send.at[j, way],
            recv_sem=f_recv.at[j, kind],
            device_id={"lat": z + 1 - 2 * way},
            device_id_type=MESH,
        )

    for t, kind, _when in sends:
        @pl.when(z == t)
        def _():
            own_copy(t, kind).wait()
    for j in range(nlat):
        @pl.when(z != j)
        def _():
            arrival(j, 0).wait_recv()
        @pl.when(has_up & (j < z))
        def _():
            pass_on(j, 0).start()
        @pl.when(has_down & (j > z))
        def _():
            pass_on(j, 1).start()
    for j in range(nlat):
        @pl.when((z != j) & has_down)
        def _():
            arrival(j, 1).wait_recv()
        @pl.when((z != j) & has_up)
        def _():
            arrival(j, 2).wait_recv()

    @pl.loop(0, rows + 2 * REACH)
    def _(q):
        near[q, pl.ds(0, ext), :] = jnp.concatenate([landed[j, q] for j in range(nlat)], axis=-1)

    nbasis = forward.shape[1] // TILE
    total[...] = jnp.zeros_like(total)

    @pl.loop(0, rows)
    def _(i):
        for tile in range(tiles):
            source = jnp.concatenate(
                [near[i + a, pl.ds(tile * TILE, WINDOW), :] for a in range(SPAN)], axis=0
            )
            made = jnp.dot(forward[i], source, preferred_element_type=jnp.float32)
            for k in range(nbasis):
                feats[i, pl.ds(tile * TILE, TILE), pl.ds(k * chs, chs)] = made[
                    k * TILE : (k + 1) * TILE
                ].astype(feats.dtype)
        held = feats[i, pl.ds(0, width), :]
        total[...] += lax.dot_general(
            held, cot[i], (((0,), (0,)), ((), ())), preferred_element_type=jnp.float32
        )

    def term(l, c, o):
        at = ((l * nchan + c) * nlon + o) * block
        return total[pl.ds(pl.multiple_of(at, 16), block), :]

    def exchange(send, recv, n, device):
        return pltpu.make_async_remote_copy(
            src_ref=send, dst_ref=recv, send_sem=g_send.at[n], recv_sem=g_recv.at[n],
            device_id=device, device_id_type=MESH,
        )

    for l in range(nlat):
        for c in range(nchan):
            send1[l, c] = term(l, c, 1 - core).astype(send1.dtype)
    over_core = exchange(send1, recv1, 0, {"lon": 1 - core})
    over_core.start()

    @pl.loop(0, rows)
    def _(i):
        out[i] = lax.dot_general(
            feats[i, pl.ds(0, width), :], mixing[...], (((1,), (1,)), ((), ())),
            preferred_element_type=jnp.float32,
        ).astype(out.dtype)

    over_core.wait()

    for l in range(nlat):
        value = term(l, 1 - x, core) + recv1[l, 1 - x].astype(jnp.float32)
        send2[l] = value.astype(send2.dtype)
    over_x = exchange(send2, recv2, 1, {"chan": 1 - x})
    over_x.start()

    @pl.when(has_down)
    def _():
        cot_copy(0).wait_recv()

    @pl.when(has_up)
    def _():
        cot_copy(1).wait_recv()

    for q in (0, 1, last, last + 1):
        feature_gradient(q)
    over_x.wait()

    def over_z(t):
        return pltpu.make_async_remote_copy(
            src_ref=send3.at[t], dst_ref=recv3.at[z], send_sem=g_send.at[2 + t],
            recv_sem=g_recv.at[2 + z], device_id={"lat": t}, device_id_type=MESH,
        )

    def reduced(t):
        return term(t, x, core) + recv1[t, x].astype(jnp.float32) + recv2[t].astype(jnp.float32)

    for t in range(nlat):
        @pl.when(z != t)
        def _():
            send3[t] = reduced(t).astype(send3.dtype)
            over_z(t).start()

    @pl.loop(0, rows)
    def _(i):
        for tile in range(tiles):
            source = jnp.concatenate(
                [
                    grads[i + q, pl.ds(tile * TILE, WINDOW), pl.ds(k * chs, chs)]
                    for q in range(SPAN)
                    for k in range(nbasis)
                ],
                axis=0,
            )
            made = jnp.dot(backward[i], source, preferred_element_type=jnp.float32)
            count = min(TILE, width - tile * TILE)
            grad_in[i, pl.ds(tile * TILE, count), :] = made[:count].astype(grad_in.dtype)

    grad_w[...] = reduced(z)
    for j in range(nlat):
        @pl.when(z != j)
        def _():
            pltpu.make_async_remote_copy(
                src_ref=send3.at[j], dst_ref=recv3.at[j], send_sem=g_send.at[2 + j],
                recv_sem=g_recv.at[2 + j], device_id={"lat": j}, device_id_type=MESH,
            ).wait_recv()
            grad_w[...] += recv3[j].astype(jnp.float32)
    grad_w[...] = grad_w[...] * factor

    for t in range(nlat):
        @pl.when(z != t)
        def _():
            over_z(t).wait_send()
    for t, kind, when in sends:
        @pl.when(when)
        def _():
            field_copy(t, kind).wait_send()
    for s in range(nshard):
        @pl.when(mine != s)
        def _():
            weight_copy(s).wait_send()
    for j in range(nlat):
        @pl.when(has_up & (j < z))
        def _():
            pass_on(j, 0).wait_send()
        @pl.when(has_down & (j > z))
        def _():
            pass_on(j, 1).wait_send()

    @pl.when(has_up)
    def _():
        cot_copy(0).wait_send()

    @pl.when(has_down)
    def _():
        cot_copy(1).wait_send()


def fused(features, basis, block_start, block_width, weight, cotangent):
    nlat, nchan, nlon = (lax.axis_size(a) for a in ("lat", "chan", "lon"))
    rows, width, chs = cotangent.shape
    part, depth = features.shape[2], weight.shape[0]
    factor = 1.0 / math.sqrt(rows * nlat * width * nchan * nlon)
    forward, backward = band_maps(basis, block_start, block_width, rows)
    field, cot_ext = ring_edges(features), ring_edges(cotangent)
    ext = field.shape[1]
    tiles = (width + TILE - 1) // TILE
    wide = max(ext, (tiles - 1) * TILE + WINDOW)
    tall, block = rows + 2 * REACH, depth // (nlat * nchan * nlon)
    half = jnp.bfloat16
    dma = pltpu.SemaphoreType.DMA
    vmem, anywhere = pl.BlockSpec(memory_space=pltpu.VMEM), pl.BlockSpec(memory_space=pl.ANY)
    return pl.pallas_call(
        functools.partial(layer_kernel, nlat, nchan, nlon, factor),
        out_shape=(
            jax.ShapeDtypeStruct((rows, width, chs), half),
            jax.ShapeDtypeStruct((rows, width, chs), half),
            jax.ShapeDtypeStruct((block, chs), jnp.float32),
        ),
        in_specs=[anywhere, anywhere, anywhere, vmem, vmem, vmem],
        out_specs=(vmem, vmem, vmem),
        scratch_shapes=[
            pltpu.VMEM((nlat, tall, ext, part), half),
            pltpu.VMEM((tall, wide, chs), half),
            pltpu.VMEM((tall, ext, chs), half),
            pltpu.VMEM((chs, depth), half),
            pltpu.VMEM((nchan * nlon, chs // (nchan * nlon), depth), half),
            pltpu.VMEM((rows, tiles * TILE, depth), half),
            pltpu.VMEM((tall, wide, depth), half),
            pltpu.VMEM((depth, chs), jnp.float32),
            pltpu.VMEM((nlat, nchan, block, chs), half),
            pltpu.VMEM((nlat, nchan, block, chs), half),
            pltpu.VMEM((nlat, block, chs), half),
            pltpu.VMEM((nlat, block, chs), half),
            pltpu.VMEM((nlat, block, chs), half),
            pltpu.VMEM((nlat, block, chs), half),
            dma((nlat, 3)),
            dma((nlat, 3)),
            dma((nlat, 2)),
            dma((nchan * nlon,)),
            dma((nchan * nlon,)),
            dma((2,)),
            dma((2,)),
            dma((5,)),
            dma((2 + nlat,)),
            dma((2 + nlat,)),
        ],
        compiler_params=pltpu.CompilerParams(
            collective_id=0, has_side_effects=True, vmem_limit_bytes=60 * 1024 * 1024
        ),
    )(field, cot_ext, weight.T, cotangent, forward, backward)


def on_device(features, basis, block_start, block_width, weight, cotangent):
    nlat, nchan, nlon = (lax.axis_size(a) for a in ("lat", "chan", "lon"))
    rows, _, chs = cotangent.shape
    shards = nchan * nlon
    tiled = chs % 128 == 0 and (chs // shards) % 16 == 0 and (weight.shape[0] // (nlat * shards)) % 16 == 0
    if tiled and nchan == 2 and nlon == 2 and nlat > 1 and rows >= REACH:
        run = fused
    else:
        run = plain
    return run(features, basis, block_start, block_width, weight, cotangent)


def solution(mesh):
    return jax.shard_map(
        on_device,
        mesh=mesh,
        in_specs=(
            P("group", ("chan", "lon"), "lat"),
            P(),
            P(),
            P(),
            P(None, ("chan", "lon")),
            P(("group", "lat"), ("chan", "lon"), None),
        ),
        out_specs=(
            P(("group", "lat"), ("chan", "lon"), None),
            P(("group", "lat"), ("chan", "lon"), None),
            P(("group", "lat", "chan", "lon"), None),
        ),
        check_vma=False,
    )
```

profile of v0, /device:TPU:0, one launch (start us, length us, event | category | flops | bytes accessed | tf_op | source)
XLA Modules:
  0.0 273.9 jit_solution(8789776465855834581)
XLA Ops:
  0.6 1.4 fusion.12
  2.5 2.0 collective-permute-start.3
  4.5 2.9 %copy.47 = bf16[16,360,160]{2,1,0:T(8,128)(2,1)S(1)} copy(bf16[16,360,160]{1,2,0:T(8,128)(2,1)} %param.6) | data formatting | bytes 3686400 | tf_op args[0]
  8.7 1.1 collective-permute-start.1
  12.1 0.7 copy.61
  24.0 1.4 broadcast_in_dim.291
  25.4 1.2 copy.96
  26.7 1.4 broadcast_in_dim.298
  28.1 1.9 copy.99
  30.0 1.4 broadcast_in_dim.305
  31.4 1.9 copy.102
  33.3 0.9 broadcast_in_dim.244
  34.2 0.8 copy.129
  35.0 1.9 copy.50
  36.9 0.9 broadcast_in_dim.252
  37.8 0.8 copy.128
  38.6 1.9 copy.53
  40.4 0.9 broadcast_in_dim.258
  41.4 0.8 copy.127
  42.1 1.9 copy.56
  44.0 0.9 broadcast_in_dim.264
  44.9 0.8 copy.126
  45.7 1.9 copy.59
  47.6 0.9 broadcast_in_dim.270
  48.5 0.8 copy.125
  49.3 1.9 copy.62
  51.1 1.9 broadcast_in_dim.250
  53.1 4.6 %broadcast_in_dim.251 = bf16[4,256,720]{1,2,0:T(8,128)(2,1)} reshape(bf16[4,2,128,5,144]{2,1,4,3,0:T(2,128)(2,1)} %broadcast_in_dim.250) | data formatting | bytes 2949120 | tf_op jit(solution)/shard_map/jit(_where)/broadcast_in_dim | solution.py:148
  57.7 2.6 copy.69
  60.3 1.9 broadcast_in_dim.256
  62.2 4.6 %broadcast_in_dim.257 = bf16[4,256,720]{1,2,0:T(8,128)(2,1)} reshape(bf16[4,2,128,5,144]{2,1,4,3,0:T(2,128)(2,1)} %broadcast_in_dim.256) | data formatting | bytes 2949120 | tf_op jit(solution)/shard_map/jit(_where)/broadcast_in_dim | solution.py:148
  66.9 2.6 copy.68
  69.4 2.0 broadcast_in_dim.262
  71.4 4.7 %broadcast_in_dim.263 = bf16[4,256,720]{1,2,0:T(8,128)(2,1)} reshape(bf16[4,2,128,5,144]{2,1,4,3,0:T(2,128)(2,1)} %broadcast_in_dim.262) | data formatting | bytes 2949120 | tf_op jit(solution)/shard_map/jit(_where)/broadcast_in_dim | solution.py:148
  76.1 2.6 copy.67
  78.7 1.9 broadcast_in_dim.268
  80.6 4.7 %broadcast_in_dim.269 = bf16[4,256,720]{1,2,0:T(8,128)(2,1)} reshape(bf16[4,2,128,5,144]{2,1,4,3,0:T(2,128)(2,1)} %broadcast_in_dim.268) | data formatting | bytes 2949120 | tf_op jit(solution)/shard_map/jit(_where)/broadcast_in_dim | solution.py:148
  85.3 2.6 copy.66
  87.9 1.9 broadcast_in_dim.274
  89.8 4.7 %broadcast_in_dim.275 = bf16[4,256,720]{1,2,0:T(8,128)(2,1)} reshape(bf16[4,2,128,5,144]{2,1,4,3,0:T(2,128)(2,1)} %broadcast_in_dim.274) | data formatting | bytes 2949120 | tf_op jit(solution)/shard_map/jit(_where)/broadcast_in_dim | solution.py:148
  94.5 2.6 copy.65
  97.1 5.9 %select_select_fusion.1.forward = bf16[4,256,720]{2,1,0:T(8,128)(2,1)} fusion(bf16[4,256,720]{2,1,0:T(8,128)(2,1)} %copy.69, bf16[4,256,720]{2,1,0:T(8,128)(2,1)} %copy.68, bf16[4,256,720]{2,1,0:T(8,128)(2,1)} %copy.67, bf16[4,256,720]{2,1,0:T(8,128)(2,1)} %copy.66, bf16[4,256,720]{2,1,0:T(8,128)(2,1)} %copy.65, pred[256,720]{1,0:T(8,128)(4,1)} %copy.62, ...), kind=kLoop, calls=%fused_computation.3 | loop fusion | flops 3686400 | bytes 9768960 | tf_op jit(solution)/shard_map/jit(_where)/select_n | solution.py:148
  103.1 2.2 select_select_fusion.backward
  105.4 2.8 %maximum_maximum_fusion.1.cot_ext = bf16[4,368,640]{2,1,0:T(8,128)(2,1)} fusion(bf16[4,2,640]{2,1,0:T(2,128)(2,1)} %collective-permute-done.3, bf16[4,360,640]{2,1,0:T(8,128)(2,1)S(1)} %copy-done, bf16[4,2,640]{2,1,0:T(2,128)(2,1)} %collective-permute-done.2, bf16[368]{0:T(512)(128)(2,1)S(1)} %pad.16.clone), kind=kLoop, calls=%fused_computation.1 | loop fusion | flops 7536640 | bytes 3748576 | tf_op jit(solution)/shard_map/concatenate | solution.py:130
  108.2 4.7 %maximum_maximum_fusion.field = bf16[16,368,160]{2,1,0:T(8,128)(2,1)} fusion(bf16[16,2,160]{2,1,0:T(2,128)(2,1)} %collective-permute-done.1, bf16[16,360,160]{2,1,0:T(8,128)(2,1)S(1)} %copy.47, bf16[16,2,160]{2,1,0:T(2,128)(2,1)} %collective-permute-done, bf16[368]{0:T(512)(128)(2,1)S(1)} %pad.16.clone), kind=kLoop, calls=%fused_computation | loop fusion | flops 7536640 | bytes 3748576 | tf_op jit(solution)/shard_map/concatenate | solution.py:130
  112.9 156.0 %shard_map.85 = (bf16[4,360,640]{2,1,0:T(8,128)(2,1)}, bf16[4,360,640]{2,1,0:T(8,128)(2,1)}, f32[80,640]{1,0:T(8,128)}) custom-call(bf16[16,368,160]{2,1,0:T(8,128)(2,1)} %maximum_maximum_fusion.field, bf16[4,368,640]{2,1,0:T(8,128)(2,1)} %maximum_maximum_fusion.1.cot_ext, bf16[160,1280]{1,0:T(8,128)(2,1)} %bitcast.125, bf16[4,360,640]{2,1,0:T(8,128)(2,1)} %cot.1, ...), custom_call_target="tpu_custom_call" | custom-call | tf_op jit(solution)/shard_map/pallas_call | solution.py:508
  268.9 3.0 %copy.149 = bf16[4,360,640]{2,1,0:T(8,128)(2,1)} copy(bf16[4,360,640]{2,1,0:T(8,128)(2,1)} %get-tuple-element.40) | data formatting | bytes 3686400
  271.9 1.2 copy.150
  (128 shorter events, 15.8 us)
Async XLA Ops:
  2.1 103.3 %collective-permute-start.2 = (bf16[4,2,640]{2,1,0:T(2,128)(2,1)}, bf16[4,2,640]{2,1,0:T(2,128)(2,1)}, u32[]{:S(2)}, u32[]{:S(2)}) collective-permute-start(bf16[4,2,640]{2,1,0:T(2,128)(2,1)} %get-tuple-element.5), channel_id=1, source_target_pairs={{0,1},{1,2},{2,3},{3,0},{4,5},{5,6},{6,7},{7,4},{8,9},{9,10},{10,1... | collective-permute-start | bytes 30728 | tf_op jit(solution)/shard_map/ppermute | solution.py:126
  2.5 9.3 %copy-start.17 = (s32[16]{0:T(128)S(1)}, s32[16]{0:T(128)}, u32[]{:S(2)}) copy-start(s32[16]{0:T(128)} %param.8) | copy-start | bytes 196
  2.5 9.3 %copy-start.18 = (s32[16]{0:T(128)S(1)}, s32[16]{0:T(128)}, u32[]{:S(2)}) copy-start(s32[16]{0:T(128)} %param.9) | copy-start | bytes 196
  2.5 9.3 %copy-start.16 = (bf16[16,2,5,5]{0,1,3,2:T(2,128)(2,1)S(1)}, bf16[16,2,5,5]{0,1,3,2:T(2,128)(2,1)}, u32[]{:S(2)}) copy-start(bf16[16,2,5,5]{0,1,3,2:T(2,128)(2,1)} %param.7) | copy-start | bytes 4804
  2.5 102.9 %collective-permute-start.3 = (bf16[4,2,640]{2,1,0:T(2,128)(2,1)}, bf16[4,2,640]{2,1,0:T(2,128)(2,1)}, u32[]{:S(2)}, u32[]{:S(2)}) collective-permute-start(bf16[4,2,640]{2,1,0:T(2,128)(2,1)} %get-tuple-element.6), channel_id=1, source_target_pairs={{1,0},{2,1},{3,2},{0,3},{5,4},{6,5},{7,6},{4,7},{9,8},{10,9},{11,1... | collective-permute-start | bytes 30728 | tf_op jit(solution)/shard_map/ppermute | solution.py:127
  8.1 100.1 %collective-permute-start = (bf16[16,2,160]{2,1,0:T(2,128)(2,1)}, bf16[16,2,160]{2,1,0:T(2,128)(2,1)}, u32[]{:S(2)}, u32[]{:S(2)}) collective-permute-start(bf16[16,2,160]{2,1,0:T(2,128)(2,1)} %get-tuple-element.3), channel_id=1, source_target_pairs={{0,1},{1,2},{2,3},{3,0},{4,5},{5,6},{6,7},{7,4},{8,9},{9,10},{10,1... | collective-permute-start | bytes 30728 | tf_op jit(solution)/shard_map/ppermute | solution.py:126
  8.7 99.4 %collective-permute-start.1 = (bf16[16,2,160]{2,1,0:T(2,128)(2,1)}, bf16[16,2,160]{2,1,0:T(2,128)(2,1)}, u32[]{:S(2)}, u32[]{:S(2)}) collective-permute-start(bf16[16,2,160]{2,1,0:T(2,128)(2,1)} %get-tuple-element.4), channel_id=1, source_target_pairs={{1,0},{2,1},{3,2},{0,3},{5,4},{6,5},{7,6},{4,7},{9,8},{10,9},{11,1... | collective-permute-start | bytes 30728 | tf_op jit(solution)/shard_map/ppermute | solution.py:127
  11.7 13.7 %copy-start.6 = (pred[128,144]{0,1:T(8,128)(4,1)}, pred[128,144]{0,1:T(8,128)(4,1)S(1)}, u32[]{:S(2)}) copy-start(pred[128,144]{0,1:T(8,128)(4,1)S(1)} %fusion.1) | copy-start | bytes 55300
  11.8 11.5 %copy-start.5 = (pred[128,144]{0,1:T(8,128)(4,1)}, pred[128,144]{0,1:T(8,128)(4,1)S(1)}, u32[]{:S(2)}) copy-start(pred[128,144]{0,1:T(8,128)(4,1)S(1)} %fusion) | copy-start | bytes 55300
  42.1 9.0 %copy-start.15 = (bf16[4,2,5]{1,2,0:T(8,128)(2,1)S(1)}, bf16[4,2,5]{1,2,0:T(8,128)(2,1)}, u32[]{:S(2)}) copy-start(bf16[4,2,5]{1,2,0:T(8,128)(2,1)} %copy.52) | copy-start | bytes 244
  57.7 2.6 copy-start.14
  66.9 2.6 copy-start.13
  76.1 2.6 copy-start.12
  97.1 6.0 %copy-start.2 = (pred[128,1440]{1,0:T(8,128)(4,1)S(1)}, pred[128,1440]{1,0:T(8,128)(4,1)}, u32[]{:S(2)}) copy-start(pred[128,1440]{1,0:T(8,128)(4,1)} %copy.99) | copy-start | bytes 552964
  97.1 6.0 %copy-start.3 = (pred[128,1440]{1,0:T(8,128)(4,1)S(1)}, pred[128,1440]{1,0:T(8,128)(4,1)}, u32[]{:S(2)}) copy-start(pred[128,1440]{1,0:T(8,128)(4,1)} %copy.102) | copy-start | bytes 552964
  97.1 6.0 %copy-start.7 = (bf16[4,1440]{1,0:T(4,128)(2,1)S(1)}, bf16[4,1440]{1,0:T(4,128)(2,1)}, u32[]{:S(2)}) copy-start(bf16[4,1440]{1,0:T(4,128)(2,1)} %broadcast_in_dim.282) | copy-start | bytes 34564
  97.1 6.0 %copy-start.8 = (bf16[4,1440]{1,0:T(4,128)(2,1)S(1)}, bf16[4,1440]{1,0:T(4,128)(2,1)}, u32[]{:S(2)}) copy-start(bf16[4,1440]{1,0:T(4,128)(2,1)} %broadcast_in_dim.310) | copy-start | bytes 34564
  97.1 6.0 %copy-start.9 = (bf16[4,1440]{1,0:T(4,128)(2,1)S(1)}, bf16[4,1440]{1,0:T(4,128)(2,1)}, u32[]{:S(2)}) copy-start(bf16[4,1440]{1,0:T(4,128)(2,1)} %broadcast_in_dim.303) | copy-start | bytes 34564
  97.1 6.0 %copy-start.10 = (bf16[4,1440]{1,0:T(4,128)(2,1)S(1)}, bf16[4,1440]{1,0:T(4,128)(2,1)}, u32[]{:S(2)}) copy-start(bf16[4,1440]{1,0:T(4,128)(2,1)} %broadcast_in_dim.296) | copy-start | bytes 34564
  97.1 6.0 %copy-start.11 = (bf16[4,1440]{1,0:T(4,128)(2,1)S(1)}, bf16[4,1440]{1,0:T(4,128)(2,1)}, u32[]{:S(2)}) copy-start(bf16[4,1440]{1,0:T(4,128)(2,1)} %broadcast_in_dim.289) | copy-start | bytes 34564
  103.1 2.3 copy-start
  268.9 3.0 %copy-start.1 = (bf16[4,360,640]{2,1,0:T(8,128)(2,1)S(1)}, bf16[4,360,640]{2,1,0:T(8,128)(2,1)}, u32[]{:S(2)}) copy-start(bf16[4,360,640]{2,1,0:T(8,128)(2,1)} %get-tuple-element.41) | copy-start | bytes 5529604
  271.9 1.2 copy-start.4
where the time goes:
time: 275 us; the launch traced here: 274 us
  Pallas kernels  156 us (57%)
  local copies, waits for them, and re-layouts  95.1 us (35%)
  other arithmetic  17.6 us (6%)
  starting transfers between devices  4.19 us (2%)
    pallas_call x1, Pallas kernels, fused(): pl.pallas_call(functools.partial(layer_kernel, nlat, nchan, nlon, factor)...  156 us
    broadcast_in_dim x31, local copies, waits for them, and re-layouts, band_maps(): forward = jnp.where(hit, own[:, :, :, b][:, :, None, :, None], forward)  63.1 us
    broadcast_in_dim x25, local copies, waits for them, and re-layouts, band_maps(): backward = jnp.where(hit, source[:, None, :, :, b, None], backward)  14.6 us
    unnamed x63, local copies, waits for them, and re-layouts  11.9 us
    concatenate x2, other arithmetic, ring_edges(): return jnp.concatenate([before, array, after, zeros], axis=1)  7.5 us
    select_n x1, other arithmetic, band_maps(): forward = jnp.where(hit, own[:, :, :, b][:, :, None, :, None], forward)  5.95 us
  transfers between devices with their start and end apart: 4, of which 0 were waited for; matrix products, arithmetic and copies ran while one was open for 37% of the time, Pallas kernels for 0%

commit v1 on v0

--- a/solution.py
+++ b/solution.py
@@ -119,58 +119,31 @@
 MESH = pl.DeviceIdType.MESH
 
 
-def ring_edges(array):
+def ring_edges(array, dim, multiple):
     axes = ("chan", "lon")
-    size, width = lax.axis_size(axes), array.shape[1]
+    size, width = lax.axis_size(axes), array.shape[dim]
     up = [(i, (i + 1) % size) for i in range(size)]
-    before = lax.ppermute(array[:, width - REACH :], axes, up)
-    after = lax.ppermute(array[:, :REACH], axes, [(j, i) for i, j in up])
-    fill = -(width + 2 * REACH) % 16
-    zeros = jnp.zeros((array.shape[0], fill, array.shape[2]), array.dtype)
-    return jnp.concatenate([before, array, after, zeros], axis=1)
-
-
-def band_maps(basis, block_start, block_width, rows):
-    column = jnp.arange(SPAN, dtype=jnp.int32)
-    valid = (column[None, :] >= block_start[:, None]) & (
-        column[None, :] < (block_start + block_width)[:, None]
-    )
-    blocks = jnp.where(valid[:, None, None, :], basis, jnp.zeros_like(basis))
-    blocks = jnp.pad(blocks, ((REACH, REACH), (0, 0), (0, 0), (0, 0)))
-    first = lax.axis_index("lat") * rows
-    near = lax.dynamic_slice_in_dim(blocks, first, rows + 2 * REACH, 0)
-    own = near[REACH : REACH + rows]
-    nbasis = basis.shape[1]
-    shift = jnp.arange(WINDOW, dtype=jnp.int32)[None, :] - jnp.arange(TILE, dtype=jnp.int32)[:, None]
-    forward = jnp.zeros((rows, nbasis, TILE, SPAN, WINDOW), basis.dtype)
-    for b in range(SPAN):
-        hit = (shift == b)[None, None, :, None, :]
-        forward = jnp.where(hit, own[:, :, :, b][:, :, None, :, None], forward)
-    source = jnp.stack(
-        [jnp.stack([near[i + q, :, SPAN - 1 - q, :] for q in range(SPAN)]) for i in range(rows)]
-    )
-    backward = jnp.zeros((rows, TILE, SPAN, nbasis, WINDOW), basis.dtype)
-    for b in range(SPAN):
-        hit = (shift == SPAN - 1 - b)[None, :, None, None, :]
-        backward = jnp.where(hit, source[:, None, :, :, b, None], backward)
-    return (
-        forward.reshape(rows, nbasis * TILE, SPAN * WINDOW),
-        backward.reshape(rows, TILE, SPAN * nbasis * WINDOW),
-    )
+    final = lax.slice_in_dim(array, width - REACH, width, axis=dim)
+    initial = lax.slice_in_dim(array, 0, REACH, axis=dim)
+    before = lax.ppermute(final, axes, up)
+    after = lax.ppermute(initial, axes, [(j, i) for i, j in up])
+    shape = list(array.shape)
+    shape[dim] = -(width + 2 * REACH) % multiple
+    return jnp.concatenate([before, array, after, jnp.zeros(shape, array.dtype)], axis=dim)
 
 
 def layer_kernel(
     nlat, nchan, nlon, factor,
-    field, cot_ext, weight_t, cot, forward, backward,
+    field, cot_ext, weight_t, cot, basis, start, count_used,
     out, grad_in, grad_w,
-    landed, near, cots, mixing, gathered, feats, grads, total,
+    forward, backward, landed, cots, mixing, gathered, feats, grads, total,
     send1, recv1, send2, recv2, send3, recv3,
     f_send, f_recv, fwd_send, w_send, w_recv, c_send, c_recv, own_sem, g_send, g_recv,
 ):
     z, x, core = lax.axis_index("lat"), lax.axis_index("chan"), lax.axis_index("lon")
     rows, width, chs = cot.shape
-    ext, part = field.shape[1], field.shape[2]
-    wide = near.shape[1]
+    ext, part, lanes = cot_ext.shape[1], field.shape[1], field.shape[2]
+    wide = grads.shape[1]
     tiles = (width + TILE - 1) // TILE
     nshard = nchan * nlon
     mine = x * nlon + core
@@ -189,6 +162,9 @@
                 barrier, inc=1, device_id={"chan": s // nlon, "lon": s % nlon}, device_id_type=MESH
             )
     pl.semaphore_wait(barrier, nlat - 1 + nshard - 1)
+
+    def channels(j):
+        return pl.ds(pl.multiple_of(j * part, 16), part)
 
     def piece(t, kind):
         if kind == 0:
@@ -201,7 +177,7 @@
         begin, at, count = piece(t, kind)
         return pltpu.make_async_remote_copy(
             src_ref=field.at[pl.ds(begin, count)],
-            dst_ref=landed.at[z, pl.ds(at, count)],
+            dst_ref=landed.at[pl.ds(at, count), channels(z), :],
             send_sem=f_send.at[t, kind],
             recv_sem=f_recv.at[z, kind],
             device_id={"lat": t},
@@ -212,7 +188,7 @@
         _, at, count = piece(1, kind)
         return pltpu.make_async_remote_copy(
             src_ref=field.at[pl.ds(0, count)],
-            dst_ref=landed.at[j, pl.ds(at, count)],
+            dst_ref=landed.at[pl.ds(at, count), channels(j), :],
             send_sem=f_send.at[0, kind],
             recv_sem=f_recv.at[j, kind],
             device_id={"lat": 0},
@@ -236,7 +212,7 @@
     def own_copy(t, kind):
         begin, at, count = piece(t, kind)
         return pltpu.make_async_copy(
-            field.at[pl.ds(begin, count)], landed.at[t, pl.ds(at, count)], own_sem.at[kind]
+            field.at[pl.ds(begin, count)], landed.at[pl.ds(at, count), channels(t), :], own_sem.at[kind]
         )
 
     for t, kind, _when in sends:
@@ -276,16 +252,7 @@
 
     has_up, has_down = z < nlat - 1, z > 0
 
-    @pl.when(has_up)
-    def _():
-        cot_copy(0).start()
-
-    @pl.when(has_down)
-    def _():
-        cot_copy(1).start()
-
     if wide > ext:
-        near[:, pl.ds(ext, wide - ext), :] = jnp.zeros((rows + 2 * REACH, wide - ext, chs), near.dtype)
         grads[:, pl.ds(ext, wide - ext), :] = jnp.zeros(
             (rows + 2 * REACH, wide - ext, grads.shape[2]), grads.dtype
         )
@@ -293,12 +260,50 @@
     @pl.when(jnp.logical_not(has_down))
     def _():
         cots[pl.ds(0, REACH)] = jnp.zeros((REACH, ext, chs), cots.dtype)
-        landed[:, pl.ds(0, REACH)] = jnp.zeros((nlat, REACH, ext, part), landed.dtype)
+        landed[pl.ds(0, REACH)] = jnp.zeros((REACH, chs, lanes), landed.dtype)
 
     @pl.when(jnp.logical_not(has_up))
     def _():
         cots[pl.ds(last, REACH)] = jnp.zeros((REACH, ext, chs), cots.dtype)
-        landed[:, pl.ds(last, REACH)] = jnp.zeros((nlat, REACH, ext, part), landed.dtype)
+        landed[pl.ds(last, REACH)] = jnp.zeros((REACH, chs, lanes), landed.dtype)
+
+    shift = lax.broadcasted_iota(jnp.int32, (TILE, WINDOW), 1) - lax.broadcasted_iota(
+        jnp.int32, (TILE, WINDOW), 0
+    )
+    total_rows = rows * nlat
+    nbasis = basis.shape[1] // (SPAN * SPAN)
+
+    def value(row, k, a, b):
+        held = jnp.clip(row, 0, total_rows - 1)
+        used = (b >= start[held]) & (b < start[held] + count_used[held])
+        used = used & (row >= 0) & (row < total_rows)
+        return jnp.where(used, basis[held, (k * SPAN + a) * SPAN + b], 0.0)
+
+    turned = lax.broadcasted_iota(jnp.int32, (2 * TILE, TILE), 0) - lax.broadcasted_iota(
+        jnp.int32, (2 * TILE, TILE), 1
+    )
+
+    def band(row, k, a, back):
+        offset = shift if back else turned
+        made = jnp.zeros(offset.shape, jnp.float32)
+        for b in range(SPAN):
+            made = jnp.where(offset == (SPAN - 1 - b if back else b), value(row, k, a, b), made)
+        return made
+
+    @pl.loop(0, rows)
+    def _(i):
+        row = z * rows + i
+        for k in range(nbasis):
+            for a in range(SPAN):
+                forward[i, a, :, pl.ds(k * TILE, TILE)] = band(row, k, a, False).astype(forward.dtype)
+        backward[i] = jnp.concatenate(
+            [
+                band(row + q - REACH, k, SPAN - 1 - q, True)
+                for q in range(SPAN)
+                for k in range(nbasis)
+            ],
+            axis=1,
+        ).astype(backward.dtype)
 
     own_weight.wait()
     for s in range(nshard):
@@ -325,8 +330,8 @@
     def pass_on(j, way):
         begin, at, kind = ((last - REACH, 0, 1), (REACH, last, 2))[way]
         return pltpu.make_async_remote_copy(
-            src_ref=landed.at[j, pl.ds(begin, REACH)],
-            dst_ref=landed.at[j, pl.ds(at, REACH)],
+            src_ref=landed.at[pl.ds(begin, REACH), channels(j), :],
+            dst_ref=landed.at[pl.ds(at, REACH), channels(j), :],
             send_sem=fwd_send.at[j, way],
             recv_sem=f_recv.at[j, kind],
             device_id={"lat": z + 1 - 2 * way},
@@ -355,27 +360,33 @@
         def _():
             arrival(j, 2).wait_recv()
 
-    @pl.loop(0, rows + 2 * REACH)
-    def _(q):
-        near[q, pl.ds(0, ext), :] = jnp.concatenate([landed[j, q] for j in range(nlat)], axis=-1)
-
-    nbasis = forward.shape[1] // TILE
+    @pl.when(has_up)
+    def _():
+        cot_copy(0).start()
+
+    @pl.when(has_down)
+    def _():
+        cot_copy(1).start()
+
     total[...] = jnp.zeros_like(total)
 
     @pl.loop(0, rows)
     def _(i):
         for tile in range(tiles):
-            source = jnp.concatenate(
-                [near[i + a, pl.ds(tile * TILE, WINDOW), :] for a in range(SPAN)], axis=0
-            )
-            made = jnp.dot(forward[i], source, preferred_element_type=jnp.float32)
+            reach = min(2 * TILE, lanes - tile * TILE)
+            made = jnp.zeros((chs, nbasis * TILE), jnp.float32)
+            for a in range(SPAN):
+                made = made + jnp.dot(
+                    landed[i + a, :, pl.ds(tile * TILE, reach)],
+                    forward[i, a, pl.ds(0, reach), :],
+                    preferred_element_type=jnp.float32,
+                )
             for k in range(nbasis):
-                feats[i, pl.ds(tile * TILE, TILE), pl.ds(k * chs, chs)] = made[
-                    k * TILE : (k + 1) * TILE
+                feats[i, pl.ds(k * chs, chs), pl.ds(tile * TILE, TILE)] = made[
+                    :, k * TILE : (k + 1) * TILE
                 ].astype(feats.dtype)
-        held = feats[i, pl.ds(0, width), :]
-        total[...] += lax.dot_general(
-            held, cot[i], (((0,), (0,)), ((), ())), preferred_element_type=jnp.float32
+        total[...] += jnp.dot(
+            feats[i, :, pl.ds(0, width)], cot[i], preferred_element_type=jnp.float32
         )
 
     def term(l, c, o):
@@ -396,10 +407,8 @@
 
     @pl.loop(0, rows)
     def _(i):
-        out[i] = lax.dot_general(
-            feats[i, pl.ds(0, width), :], mixing[...], (((1,), (1,)), ((), ())),
-            preferred_element_type=jnp.float32,
-        ).astype(out.dtype)
+        mixed = jnp.dot(mixing[...], feats[i], preferred_element_type=jnp.float32)
+        out[i] = mixed.T[:width].astype(out.dtype)
 
     over_core.wait()
 
@@ -496,14 +505,17 @@
     rows, width, chs = cotangent.shape
     part, depth = features.shape[2], weight.shape[0]
     factor = 1.0 / math.sqrt(rows * nlat * width * nchan * nlon)
-    forward, backward = band_maps(basis, block_start, block_width, rows)
-    field, cot_ext = ring_edges(features), ring_edges(cotangent)
-    ext = field.shape[1]
+    nbasis = basis.shape[1]
+    table = basis.astype(jnp.float32).reshape(basis.shape[0], -1)
+    field = ring_edges(jnp.swapaxes(features, 1, 2), 2, TILE)
+    cot_ext = ring_edges(cotangent, 1, 16)
+    ext, lanes = cot_ext.shape[1], field.shape[2]
     tiles = (width + TILE - 1) // TILE
     wide = max(ext, (tiles - 1) * TILE + WINDOW)
     tall, block = rows + 2 * REACH, depth // (nlat * nchan * nlon)
     half = jnp.bfloat16
     dma = pltpu.SemaphoreType.DMA
+    smem = pl.BlockSpec(memory_space=pltpu.SMEM)
     vmem, anywhere = pl.BlockSpec(memory_space=pltpu.VMEM), pl.BlockSpec(memory_space=pl.ANY)
     return pl.pallas_call(
         functools.partial(layer_kernel, nlat, nchan, nlon, factor),
@@ -512,15 +524,16 @@
             jax.ShapeDtypeStruct((rows, width, chs), half),
             jax.ShapeDtypeStruct((block, chs), jnp.float32),
         ),
-        in_specs=[anywhere, anywhere, anywhere, vmem, vmem, vmem],
+        in_specs=[anywhere, anywhere, anywhere, vmem, smem, smem, smem],
         out_specs=(vmem, vmem, vmem),
         scratch_shapes=[
-            pltpu.VMEM((nlat, tall, ext, part), half),
-            pltpu.VMEM((tall, wide, chs), half),
+            pltpu.VMEM((rows, SPAN, 2 * TILE, nbasis * TILE), half),
+            pltpu.VMEM((rows, TILE, SPAN * nbasis * WINDOW), half),
+            pltpu.VMEM((tall, chs, lanes), half),
             pltpu.VMEM((tall, ext, chs), half),
             pltpu.VMEM((chs, depth), half),
             pltpu.VMEM((nchan * nlon, chs // (nchan * nlon), depth), half),
-            pltpu.VMEM((rows, tiles * TILE, depth), half),
+            pltpu.VMEM((rows, depth, tiles * TILE), half),
             pltpu.VMEM((tall, wide, depth), half),
             pltpu.VMEM((depth, chs), jnp.float32),
             pltpu.VMEM((nlat, nchan, block, chs), half),
@@ -543,15 +556,15 @@
         compiler_params=pltpu.CompilerParams(
             collective_id=0, has_side_effects=True, vmem_limit_bytes=60 * 1024 * 1024
         ),
-    )(field, cot_ext, weight.T, cotangent, forward, backward)
+    )(field, cot_ext, weight.T, cotangent, table, block_start, block_width)
 
 
 def on_device(features, basis, block_start, block_width, weight, cotangent):
     nlat, nchan, nlon = (lax.axis_size(a) for a in ("lat", "chan", "lon"))
     rows, _, chs = cotangent.shape
     shards = nchan * nlon
-    tiled = chs % 128 == 0 and (chs // shards) % 16 == 0 and (weight.shape[0] // (nlat * shards)) % 16 == 0
-    if tiled and nchan == 2 and nlon == 2 and nlat > 1 and rows >= REACH:
+    tiled = chs % 128 == 0 and (chs // shards) % 16 == 0 and (chs // nlat) % 16 == 0 and (weight.shape[0] // (nlat * shards)) % 16 == 0
+    if tiled and features.shape[2] * nlat == chs and nchan == 2 and nlon == 2 and nlat > 1 and rows >= REACH:
         run = fused
     else:
         run = plain

time: 275 us -> 125 us (0.45)
  local copies, waits for them, and re-layouts: 95.1 us -> 9 us
  Pallas kernels: 156 us -> 104 us
  other arithmetic: 17.6 us -> 6.39 us
    broadcast_in_dim x57 -> x2, local copies, waits for them, and re-layouts: 77.7 us -> 0.01 us  [ring_edges(): jnp.zeros(shape, array.dtype)]
    pallas_call x1, Pallas kernels: 156 us -> 104 us  [fused(): pl.pallas_call(functools.partial(layer_kernel, nlat, nchan, nlon, factor)...]
    select_n x3 -> x0, other arithmetic: 8.13 us -> none  [the longest x1 5.95 us: band_maps(): forward = jnp.where(hit, own[:, :, :, b][:, :, None, :, None], forward)]
    unnamed x63 -> x11, local copies, waits for them, and re-layouts: 11.9 us -> 4.96 us
    slice x29 -> x4, local copies, waits for them, and re-layouts: 5.38 us -> 2.46 us  [the longest x3 2.07 us: ring_edges(): final = lax.slice_in_dim(array, width - REACH, width, axis=dim)]
  transfers between devices with their start and end apart: 4 -> 4, of which waited for: 0 -> 1; matrix products, arithmetic and copies ran while one was open for 37% -> 5% of each run, Pallas kernels for 0% -> 0%
where the time goes in v1:
time: 125 us
  Pallas kernels  104 us (83%)
  local copies, waits for them, and re-layouts  9 us (7%)
  other arithmetic  6.39 us (5%)
  starting transfers between devices  4.31 us (3%)
    pallas_call x1, Pallas kernels, fused(): pl.pallas_call(functools.partial(layer_kernel, nlat, nchan, nlon, factor)...  104 us
    concatenate x2, other arithmetic, ring_edges(): jnp.concatenate([before, array, after, jnp.zeros(shape, array.dtype)], ax...  6.39 us
    unnamed x11, local copies, waits for them, and re-layouts  4.96 us
    ppermute x2, starting transfers between devices, ring_edges(): after = lax.ppermute(initial, axes, [(j, i) for i, j in up])  3.54 us
  transfers between devices with their start and end apart: 4, of which 1 were waited for; matrix products, arithmetic and copies ran while one was open for 5% of the time, Pallas kernels for 0%

profile of v1, /device:TPU:0, one launch (start us, length us, event | category | flops | bytes accessed | tf_op | source)
XLA Modules:
  0.0 124.5 jit_solution(4789850310508712945)
XLA Ops:
  0.6 0.0 copy-start
  0.6 0.0 copy-start.3
  0.7 1.7 %fusion = (bf16[16,160,2]{2,1,0:T(8,128)(2,1)S(1)}, bf16[16,160,2]{2,1,0:T(8,128)(2,1)S(1)}) fusion(bf16[16,160,360]{2,1,0:T(8,128)(2,1)} %bitcast.4), kind=kLoop, calls=%fused_computation.2 | loop fusion | bytes 40960 | tf_op jit(solution)/shard_map/slice | solution.py:126
  2.3 0.4 copy.13
  2.7 2.4 %collective-permute-start.1 = (bf16[16,160,2]{1,0,2:T(8,128)(2,1)S(1)}, bf16[16,160,2]{1,0,2:T(8,128)(2,1)S(1)}, u32[]{:S(2)}, u32[]{:S(2)}) collective-permute-start(bf16[16,160,2]{1,0,2:T(8,128)(2,1)S(1)} %copy.13), channel_id=1, source_target_pairs={{1,0},{2,1},{3,2},{0,3},{5,4},{6,5},{7,6},{4,7},{9,8},{10,9},{11,1... | collective-permute-start | bytes 30728 | tf_op jit(solution)/shard_map/ppermute | solution.py:129
  5.1 0.4 copy.12
  5.5 0.0 collective-permute-start
  5.6 0.0 copy-done
  5.6 0.7 collective-permute-start.2
  6.3 1.1 collective-permute-start.3
  7.5 0.1 pad.3.clone
  7.5 0.1 pad.7.clone
  7.6 0.0 copy-done.3
  7.6 0.7 copy.17.basis
  8.3 0.4 collective-permute-done
  8.7 0.4 copy.14
  9.1 0.0 collective-permute-done.1
  9.1 0.4 copy.15
  9.5 4.3 %maximum_maximum_fusion.field = bf16[16,160,384]{2,1,0:T(8,128)(2,1)} fusion(bf16[16,160,2]{2,1,0:T(8,128)(2,1)S(1)} %copy.15, bf16[16,160,360]{2,1,0:T(8,128)(2,1)} %bitcast.5, bf16[16,160,2]{2,1,0:T(8,128)(2,1)S(1)} %copy.14, bf16[384]{0:T(512)(128)(2,1)S(1)} %pad.7.clone), kind=kLoop, calls=%fused_computation | loop fusion | flops 7864320 | bytes 3830528 | tf_op jit(solution)/shard_map/concatenate | solution.py:132
  13.8 0.0 collective-permute-done.2
  13.8 0.0 collective-permute-done.3
  13.8 2.0 %maximum_maximum_fusion.1.cot_ext = bf16[4,368,640]{2,1,0:T(8,128)(2,1)} fusion(bf16[4,2,640]{2,1,0:T(2,128)(2,1)S(1)} %collective-permute-done.3, bf16[4,360,640]{2,1,0:T(8,128)(2,1)S(1)} %copy-done, bf16[4,2,640]{2,1,0:T(2,128)(2,1)S(1)} %collective-permute-done.2, bf16[368]{0:T(512)(128)(2,1)S(1)} %pad.3.clone), kind=kLoop, calls=%fused_computation.1 | loop fusion | flops 7536640 | bytes 3748576 | tf_op jit(solution)/shard_map/concatenate | solution.py:132
  15.9 103.7 %shard_map.85 = (bf16[4,360,640]{2,1,0:T(8,128)(2,1)}, bf16[4,360,640]{2,1,0:T(8,128)(2,1)}, f32[80,640]{1,0:T(8,128)}) custom-call(bf16[16,160,384]{2,1,0:T(8,128)(2,1)} %maximum_maximum_fusion.field, bf16[4,368,640]{2,1,0:T(8,128)(2,1)} %maximum_maximum_fusion.1.cot_ext, bf16[160,1280]{1,0:T(8,128)(2,1)} %bitcast.6, bf16[4,360,640]{2,1,0:T(8,128)(2,1)} %cot.1, ...), custom_call_target="tpu_custom_call" | custom-call | tf_op jit(solution)/shard_map/pallas_call | solution.py:520
  119.6 0.0 copy-start.1
  119.6 3.0 %copy.21 = bf16[4,360,640]{2,1,0:T(8,128)(2,1)} copy(bf16[4,360,640]{2,1,0:T(8,128)(2,1)} %get-tuple-element.10) | data formatting | bytes 3686400
  122.6 0.0 copy-done.1
  122.6 0.0 copy-start.2
  122.6 1.2 copy.22
  123.8 0.0 copy-done.2
  123.8 0.7 copy.23
  (5 shorter events, 0.0 us)
Async XLA Ops:
  0.6 4.9 %copy-start = (bf16[4,360,640]{2,1,0:T(8,128)(2,1)S(1)}, bf16[4,360,640]{2,1,0:T(8,128)(2,1)}, u32[]{:S(2)}) copy-start(bf16[4,360,640]{2,1,0:T(8,128)(2,1)} %cot.1) | copy-start | bytes 5529604
  0.6 7.0 %copy-start.3 = (bf16[16,2,5,5]{0,1,3,2:T(2,128)(2,1)S(1)}, bf16[16,2,5,5]{0,1,3,2:T(2,128)(2,1)}, u32[]{:S(2)}) copy-start(bf16[16,2,5,5]{0,1,3,2:T(2,128)(2,1)} %param.7) | copy-start | bytes 4804
  2.7 6.4 %collective-permute-start.1 = (bf16[16,160,2]{1,0,2:T(8,128)(2,1)S(1)}, bf16[16,160,2]{1,0,2:T(8,128)(2,1)S(1)}, u32[]{:S(2)}, u32[]{:S(2)}) collective-permute-start(bf16[16,160,2]{1,0,2:T(8,128)(2,1)S(1)} %copy.13), channel_id=1, source_target_pairs={{1,0},{2,1},{3,2},{0,3},{5,4},{6,5},{7,6},{4,7},{9,8},{10,9},{11,1... | collective-permute-start | bytes 30728 | tf_op jit(solution)/shard_map/ppermute | solution.py:129
  5.5 3.2 %collective-permute-start = (bf16[16,160,2]{1,0,2:T(8,128)(2,1)S(1)}, bf16[16,160,2]{1,0,2:T(8,128)(2,1)S(1)}, u32[]{:S(2)}, u32[]{:S(2)}) collective-permute-start(bf16[16,160,2]{1,0,2:T(8,128)(2,1)S(1)} %copy.12), channel_id=1, source_target_pairs={{0,1},{1,2},{2,3},{3,0},{4,5},{5,6},{6,7},{7,4},{8,9},{9,10},{10,1... | collective-permute-start | bytes 30728 | tf_op jit(solution)/shard_map/ppermute | solution.py:128
  5.6 8.2 %collective-permute-start.2 = (bf16[4,2,640]{2,1,0:T(2,128)(2,1)S(1)}, bf16[4,2,640]{2,1,0:T(2,128)(2,1)S(1)}, u32[]{:S(2)}, u32[]{:S(2)}) collective-permute-start(bf16[4,2,640]{2,1,0:T(2,128)(2,1)S(1)} %get-tuple-element.5), channel_id=1, source_target_pairs={{0,1},{1,2},{2,3},{3,0},{4,5},{5,6},{6,7},{7,4},{8,9},{9,10},{10,1... | collective-permute-start | bytes 30728 | tf_op jit(solution)/shard_map/ppermute | solution.py:128
  6.3 7.5 %collective-permute-start.3 = (bf16[4,2,640]{2,1,0:T(2,128)(2,1)S(1)}, bf16[4,2,640]{2,1,0:T(2,128)(2,1)S(1)}, u32[]{:S(2)}, u32[]{:S(2)}) collective-permute-start(bf16[4,2,640]{2,1,0:T(2,128)(2,1)S(1)} %get-tuple-element.6), channel_id=1, source_target_pairs={{1,0},{2,1},{3,2},{0,3},{5,4},{6,5},{7,6},{4,7},{9,8},{10,9},{11,1... | collective-permute-start | bytes 30728 | tf_op jit(solution)/shard_map/ppermute | solution.py:129
  119.6 3.0 %copy-start.1 = (bf16[4,360,640]{2,1,0:T(8,128)(2,1)S(1)}, bf16[4,360,640]{2,1,0:T(8,128)(2,1)}, u32[]{:S(2)}) copy-start(bf16[4,360,640]{2,1,0:T(8,128)(2,1)} %get-tuple-element.11) | copy-start | bytes 5529604
  122.6 1.2 copy-start.2

commit v2 on v1

--- a/solution.py
+++ b/solution.py
@@ -136,7 +136,7 @@
     nlat, nchan, nlon, factor,
     field, cot_ext, weight_t, cot, basis, start, count_used,
     out, grad_in, grad_w,
-    forward, backward, landed, cots, mixing, gathered, feats, grads, total,
+    forward, backward, backward_far, padded_cot, held, landed, cots, mixing, gathered, feats, grads, total,
     send1, recv1, send2, recv2, send3, recv3,
     f_send, f_recv, fwd_send, w_send, w_recv, c_send, c_recv, own_sem, g_send, g_recv,
 ):
@@ -145,6 +145,7 @@
     ext, part, lanes = cot_ext.shape[1], field.shape[1], field.shape[2]
     wide = grads.shape[1]
     tiles = (width + TILE - 1) // TILE
+    lanes_out = tiles * TILE
     nshard = nchan * nlon
     mine = x * nlon + core
     block = grad_w.shape[0]
@@ -246,7 +247,7 @@
             dst_ref=cots.at[pl.ds(at, REACH)],
             send_sem=c_send.at[way],
             recv_sem=c_recv.at[way],
-            device_id={"lat": z + 1 - 2 * way},
+            device_id={"lat": lax.rem(z + 1 - 2 * way + nlat, nlat)},
             device_id_type=MESH,
         )
 
@@ -295,15 +296,31 @@
         row = z * rows + i
         for k in range(nbasis):
             for a in range(SPAN):
-                forward[i, a, :, pl.ds(k * TILE, TILE)] = band(row, k, a, False).astype(forward.dtype)
-        backward[i] = jnp.concatenate(
-            [
-                band(row + q - REACH, k, SPAN - 1 - q, True)
-                for q in range(SPAN)
-                for k in range(nbasis)
-            ],
-            axis=1,
-        ).astype(backward.dtype)
+                forward[i, pl.ds(a * 2 * TILE, 2 * TILE), pl.ds(k * TILE, TILE)] = band(
+                    row, k, a, False
+                ).astype(forward.dtype)
+
+    def sources(i, here):
+        return [q for q in range(SPAN) if (REACH <= i + q < last) == here]
+
+    for i in range(rows):
+        for here, maps in ((True, backward), (False, backward_far)):
+            made = jnp.concatenate(
+                [
+                    band(z * rows + i + q - REACH, k, SPAN - 1 - q, True)
+                    for q in sources(i, here)
+                    for k in range(nbasis)
+                ],
+                axis=1,
+            )
+            maps[i, :, pl.ds(0, made.shape[1])] = made.astype(maps.dtype)
+
+    for i in range(rows):
+        padded_cot[pl.ds(i * lanes_out, width), :] = cot[i]
+        if lanes_out > width:
+            padded_cot[pl.ds(i * lanes_out + width, lanes_out - width), :] = jnp.zeros(
+                (lanes_out - width, chs), padded_cot.dtype
+            )
 
     own_weight.wait()
     for s in range(nshard):
@@ -326,6 +343,23 @@
     @pl.loop(REACH, last)
     def _(q):
         feature_gradient(q)
+
+    def back_part(i, tile, here, maps):
+        source = jnp.concatenate(
+            [
+                grads[i + q, pl.ds(tile * TILE, WINDOW), pl.ds(k * chs, chs)]
+                for q in sources(i, here)
+                for k in range(nbasis)
+            ],
+            axis=0,
+        )
+        return jnp.dot(
+            maps[i, :, pl.ds(0, source.shape[0])], source, preferred_element_type=jnp.float32
+        )
+
+    for i in range(rows):
+        for tile in range(tiles):
+            held[i, pl.ds(tile * TILE, TILE), :] = back_part(i, tile, True, backward)
 
     def pass_on(j, way):
         begin, at, kind = ((last - REACH, 0, 1), (REACH, last, 2))[way]
@@ -352,6 +386,14 @@
         @pl.when(has_down & (j > z))
         def _():
             pass_on(j, 1).start()
+    @pl.when(has_up)
+    def _():
+        cot_copy(0).start()
+
+    @pl.when(has_down)
+    def _():
+        cot_copy(1).start()
+
     for j in range(nlat):
         @pl.when((z != j) & has_down)
         def _():
@@ -360,33 +402,29 @@
         def _():
             arrival(j, 2).wait_recv()
 
-    @pl.when(has_up)
-    def _():
-        cot_copy(0).start()
-
-    @pl.when(has_down)
-    def _():
-        cot_copy(1).start()
-
-    total[...] = jnp.zeros_like(total)
 
     @pl.loop(0, rows)
     def _(i):
         for tile in range(tiles):
             reach = min(2 * TILE, lanes - tile * TILE)
-            made = jnp.zeros((chs, nbasis * TILE), jnp.float32)
-            for a in range(SPAN):
-                made = made + jnp.dot(
-                    landed[i + a, :, pl.ds(tile * TILE, reach)],
-                    forward[i, a, pl.ds(0, reach), :],
-                    preferred_element_type=jnp.float32,
+            source = jnp.concatenate(
+                [landed[i + a, :, pl.ds(tile * TILE, reach)] for a in range(SPAN)], axis=1
+            )
+            maps = jnp.concatenate(
+                [forward[i, pl.ds(a * 2 * TILE, reach), :] for a in range(SPAN)], axis=0
+            )
+            made = jnp.dot(source, maps, preferred_element_type=jnp.float32)
+            at = pl.ds(pl.multiple_of(i * lanes_out + tile * TILE, TILE), TILE)
+            for k in range(nbasis):
+                feats[pl.ds(k * chs, chs), at] = made[:, k * TILE : (k + 1) * TILE].astype(
+                    feats.dtype
                 )
-            for k in range(nbasis):
-                feats[i, pl.ds(k * chs, chs), pl.ds(tile * TILE, TILE)] = made[
-                    :, k * TILE : (k + 1) * TILE
-                ].astype(feats.dtype)
-        total[...] += jnp.dot(
-            feats[i, :, pl.ds(0, width)], cot[i], preferred_element_type=jnp.float32
+
+    @pl.loop(0, total.shape[0] // TILE)
+    def _(n):
+        at = pl.ds(pl.multiple_of(n * TILE, TILE), TILE)
+        total[at, :] = jnp.dot(
+            feats[at, :], padded_cot[...], preferred_element_type=jnp.float32
         )
 
     def term(l, c, o):
@@ -407,7 +445,8 @@
 
     @pl.loop(0, rows)
     def _(i):
-        mixed = jnp.dot(mixing[...], feats[i], preferred_element_type=jnp.float32)
+        at = pl.ds(pl.multiple_of(i * lanes_out, TILE), lanes_out)
+        mixed = jnp.dot(mixing[...], feats[:, at], preferred_element_type=jnp.float32)
         out[i] = mixed.T[:width].astype(out.dtype)
 
     over_core.wait()
@@ -418,16 +457,6 @@
     over_x = exchange(send2, recv2, 1, {"chan": 1 - x})
     over_x.start()
 
-    @pl.when(has_down)
-    def _():
-        cot_copy(0).wait_recv()
-
-    @pl.when(has_up)
-    def _():
-        cot_copy(1).wait_recv()
-
-    for q in (0, 1, last, last + 1):
-        feature_gradient(q)
     over_x.wait()
 
     def over_z(t):
@@ -445,18 +474,21 @@
             send3[t] = reduced(t).astype(send3.dtype)
             over_z(t).start()
 
-    @pl.loop(0, rows)
-    def _(i):
+    @pl.when(has_down)
+    def _():
+        cot_copy(0).wait_recv()
+
+    @pl.when(has_up)
+    def _():
+        cot_copy(1).wait_recv()
+
+    for q in (0, 1, last, last + 1):
+        feature_gradient(q)
+    for i in range(rows):
         for tile in range(tiles):
-            source = jnp.concatenate(
-                [
-                    grads[i + q, pl.ds(tile * TILE, WINDOW), pl.ds(k * chs, chs)]
-                    for q in range(SPAN)
-                    for k in range(nbasis)
-                ],
-                axis=0,
-            )
-            made = jnp.dot(backward[i], source, preferred_element_type=jnp.float32)
+            made = held[i, pl.ds(tile * TILE, TILE), :]
+            if sources(i, False):
+                made = made + back_part(i, tile, False, backward_far)
             count = min(TILE, width - tile * TILE)
             grad_in[i, pl.ds(tile * TILE, count), :] = made[:count].astype(grad_in.dtype)
 
@@ -527,13 +559,16 @@
         in_specs=[anywhere, anywhere, anywhere, vmem, smem, smem, smem],
         out_specs=(vmem, vmem, vmem),
         scratch_shapes=[
-            pltpu.VMEM((rows, SPAN, 2 * TILE, nbasis * TILE), half),
+            pltpu.VMEM((rows, SPAN * 2 * TILE, nbasis * TILE), half),
             pltpu.VMEM((rows, TILE, SPAN * nbasis * WINDOW), half),
+            pltpu.VMEM((rows, TILE, SPAN * nbasis * WINDOW), half),
+            pltpu.VMEM((rows * tiles * TILE, chs), half),
+            pltpu.VMEM((rows, tiles * TILE, chs), jnp.float32),
             pltpu.VMEM((tall, chs, lanes), half),
             pltpu.VMEM((tall, ext, chs), half),
             pltpu.VMEM((chs, depth), half),
             pltpu.VMEM((nchan * nlon, chs // (nchan * nlon), depth), half),
-            pltpu.VMEM((rows, depth, tiles * TILE), half),
+            pltpu.VMEM((depth, rows * tiles * TILE), half),
             pltpu.VMEM((tall, wide, depth), half),
             pltpu.VMEM((depth, chs), jnp.float32),
             pltpu.VMEM((nlat, nchan, block, chs), half),
@@ -563,7 +598,7 @@
     nlat, nchan, nlon = (lax.axis_size(a) for a in ("lat", "chan", "lon"))
     rows, _, chs = cotangent.shape
     shards = nchan * nlon
-    tiled = chs % 128 == 0 and (chs // shards) % 16 == 0 and (chs // nlat) % 16 == 0 and (weight.shape[0] // (nlat * shards)) % 16 == 0
+    tiled = chs % 128 == 0 and weight.shape[0] % TILE == 0 and (chs // shards) % 16 == 0 and (chs // nlat) % 16 == 0 and (weight.shape[0] // (nlat * shards)) % 16 == 0
     if tiled and features.shape[2] * nlat == chs and nchan == 2 and nlon == 2 and nlat > 1 and rows >= REACH:
         run = fused
     else:

time: 125 us -> 122 us (0.976)
  Pallas kernels: 104 us -> 101 us
    pallas_call x1, Pallas kernels: 104 us -> 101 us  [fused(): pl.pallas_call(functools.partial(layer_kernel, nlat, nchan, nlon, factor)...]
where the time goes in v2:
time: 122 us
  Pallas kernels  101 us (83%)
  local copies, waits for them, and re-layouts  9 us (7%)
  other arithmetic  6.39 us (5%)
  starting transfers between devices  4.31 us (4%)
    pallas_call x1, Pallas kernels, fused(): pl.pallas_call(functools.partial(layer_kernel, nlat, nchan, nlon, factor)...  101 us
    concatenate x2, other arithmetic, ring_edges(): jnp.concatenate([before, array, after, jnp.zeros(shape, array.dtype)], ax...  6.39 us
    unnamed x11, local copies, waits for them, and re-layouts  4.96 us
    ppermute x2, starting transfers between devices, ring_edges(): after = lax.ppermute(initial, axes, [(j, i) for i, j in up])  3.54 us
  transfers between devices with their start and end apart: 4, of which 1 were waited for; matrix products, arithmetic and copies ran while one was open for 5% of the time, Pallas kernels for 0%

profile of v2, /device:TPU:0, one launch (start us, length us, event | category | flops | bytes accessed | tf_op | source)
XLA Modules:
  0.0 122.3 jit_solution(261204044888488306)
XLA Ops:
  0.6 0.0 copy-start
  0.6 0.0 copy-start.3
  0.7 1.7 %fusion = (bf16[16,160,2]{2,1,0:T(8,128)(2,1)S(1)}, bf16[16,160,2]{2,1,0:T(8,128)(2,1)S(1)}) fusion(bf16[16,160,360]{2,1,0:T(8,128)(2,1)} %bitcast.4), kind=kLoop, calls=%fused_computation.2 | loop fusion | bytes 40960 | tf_op jit(solution)/shard_map/slice | solution.py:126
  2.3 0.4 copy.13
  2.7 2.4 %collective-permute-start.1 = (bf16[16,160,2]{1,0,2:T(8,128)(2,1)S(1)}, bf16[16,160,2]{1,0,2:T(8,128)(2,1)S(1)}, u32[]{:S(2)}, u32[]{:S(2)}) collective-permute-start(bf16[16,160,2]{1,0,2:T(8,128)(2,1)S(1)} %copy.13), channel_id=1, source_target_pairs={{1,0},{2,1},{3,2},{0,3},{5,4},{6,5},{7,6},{4,7},{9,8},{10,9},{11,1... | collective-permute-start | bytes 30728 | tf_op jit(solution)/shard_map/ppermute | solution.py:129
  5.1 0.4 copy.12
  5.5 0.0 collective-permute-start
  5.6 0.0 copy-done
  5.6 0.7 collective-permute-start.2
  6.3 1.1 collective-permute-start.3
  7.5 0.1 pad.3.clone
  7.5 0.1 pad.7.clone
  7.6 0.0 copy-done.3
  7.6 0.7 copy.17.basis
  8.3 0.4 collective-permute-done
  8.7 0.4 copy.14
  9.1 0.0 collective-permute-done.1
  9.1 0.4 copy.15
  9.5 4.3 %maximum_maximum_fusion.field = bf16[16,160,384]{2,1,0:T(8,128)(2,1)} fusion(bf16[16,160,2]{2,1,0:T(8,128)(2,1)S(1)} %copy.15, bf16[16,160,360]{2,1,0:T(8,128)(2,1)} %bitcast.5, bf16[16,160,2]{2,1,0:T(8,128)(2,1)S(1)} %copy.14, bf16[384]{0:T(512)(128)(2,1)S(1)} %pad.7.clone), kind=kLoop, calls=%fused_computation | loop fusion | flops 7864320 | bytes 3830528 | tf_op jit(solution)/shard_map/concatenate | solution.py:132
  13.8 0.0 collective-permute-done.2
  13.8 0.0 collective-permute-done.3
  13.8 2.0 %maximum_maximum_fusion.1.cot_ext = bf16[4,368,640]{2,1,0:T(8,128)(2,1)} fusion(bf16[4,2,640]{2,1,0:T(2,128)(2,1)S(1)} %collective-permute-done.3, bf16[4,360,640]{2,1,0:T(8,128)(2,1)S(1)} %copy-done, bf16[4,2,640]{2,1,0:T(2,128)(2,1)S(1)} %collective-permute-done.2, bf16[368]{0:T(512)(128)(2,1)S(1)} %pad.3.clone), kind=kLoop, calls=%fused_computation.1 | loop fusion | flops 7536640 | bytes 3748576 | tf_op jit(solution)/shard_map/concatenate | solution.py:132
  15.9 101.4 %shard_map.85 = (bf16[4,360,640]{2,1,0:T(8,128)(2,1)}, bf16[4,360,640]{2,1,0:T(8,128)(2,1)}, f32[80,640]{1,0:T(8,128)}) custom-call(bf16[16,160,384]{2,1,0:T(8,128)(2,1)} %maximum_maximum_fusion.field, bf16[4,368,640]{2,1,0:T(8,128)(2,1)} %maximum_maximum_fusion.1.cot_ext, bf16[160,1280]{1,0:T(8,128)(2,1)} %bitcast.6, bf16[4,360,640]{2,1,0:T(8,128)(2,1)} %cot.1, ...), custom_call_target="tpu_custom_call" | custom-call | tf_op jit(solution)/shard_map/pallas_call | solution.py:552
  117.3 0.0 copy-start.1
  117.3 3.0 %copy.21 = bf16[4,360,640]{2,1,0:T(8,128)(2,1)} copy(bf16[4,360,640]{2,1,0:T(8,128)(2,1)} %get-tuple-element.10) | data formatting | bytes 3686400
  120.3 0.0 copy-done.1
  120.3 0.0 copy-start.2
  120.3 1.2 %copy.22 = bf16[4,360,640]{2,1,0:T(8,128)(2,1)} copy(bf16[4,360,640]{2,1,0:T(8,128)(2,1)S(1)} %copy-done.1) | data formatting | bytes 3686400
  121.6 0.0 copy-done.2
  121.6 0.7 copy.23
  (5 shorter events, 0.0 us)
Async XLA Ops:
  0.6 4.9 %copy-start = (bf16[4,360,640]{2,1,0:T(8,128)(2,1)S(1)}, bf16[4,360,640]{2,1,0:T(8,128)(2,1)}, u32[]{:S(2)}) copy-start(bf16[4,360,640]{2,1,0:T(8,128)(2,1)} %cot.1) | copy-start | bytes 5529604
  0.6 7.0 %copy-start.3 = (bf16[16,2,5,5]{0,1,3,2:T(2,128)(2,1)S(1)}, bf16[16,2,5,5]{0,1,3,2:T(2,128)(2,1)}, u32[]{:S(2)}) copy-start(bf16[16,2,5,5]{0,1,3,2:T(2,128)(2,1)} %param.7) | copy-start | bytes 4804
  2.7 6.4 %collective-permute-start.1 = (bf16[16,160,2]{1,0,2:T(8,128)(2,1)S(1)}, bf16[16,160,2]{1,0,2:T(8,128)(2,1)S(1)}, u32[]{:S(2)}, u32[]{:S(2)}) collective-permute-start(bf16[16,160,2]{1,0,2:T(8,128)(2,1)S(1)} %copy.13), channel_id=1, source_target_pairs={{1,0},{2,1},{3,2},{0,3},{5,4},{6,5},{7,6},{4,7},{9,8},{10,9},{11,1... | collective-permute-start | bytes 30728 | tf_op jit(solution)/shard_map/ppermute | solution.py:129
  5.5 3.2 %collective-permute-start = (bf16[16,160,2]{1,0,2:T(8,128)(2,1)S(1)}, bf16[16,160,2]{1,0,2:T(8,128)(2,1)S(1)}, u32[]{:S(2)}, u32[]{:S(2)}) collective-permute-start(bf16[16,160,2]{1,0,2:T(8,128)(2,1)S(1)} %copy.12), channel_id=1, source_target_pairs={{0,1},{1,2},{2,3},{3,0},{4,5},{5,6},{6,7},{7,4},{8,9},{9,10},{10,1... | collective-permute-start | bytes 30728 | tf_op jit(solution)/shard_map/ppermute | solution.py:128
  5.6 8.2 %collective-permute-start.2 = (bf16[4,2,640]{2,1,0:T(2,128)(2,1)S(1)}, bf16[4,2,640]{2,1,0:T(2,128)(2,1)S(1)}, u32[]{:S(2)}, u32[]{:S(2)}) collective-permute-start(bf16[4,2,640]{2,1,0:T(2,128)(2,1)S(1)} %get-tuple-element.5), channel_id=1, source_target_pairs={{0,1},{1,2},{2,3},{3,0},{4,5},{5,6},{6,7},{7,4},{8,9},{9,10},{10,1... | collective-permute-start | bytes 30728 | tf_op jit(solution)/shard_map/ppermute | solution.py:128
  6.3 7.5 %collective-permute-start.3 = (bf16[4,2,640]{2,1,0:T(2,128)(2,1)S(1)}, bf16[4,2,640]{2,1,0:T(2,128)(2,1)S(1)}, u32[]{:S(2)}, u32[]{:S(2)}) collective-permute-start(bf16[4,2,640]{2,1,0:T(2,128)(2,1)S(1)} %get-tuple-element.6), channel_id=1, source_target_pairs={{1,0},{2,1},{3,2},{0,3},{5,4},{6,5},{7,6},{4,7},{9,8},{10,9},{11,1... | collective-permute-start | bytes 30728 | tf_op jit(solution)/shard_map/ppermute | solution.py:129
  117.3 3.0 %copy-start.1 = (bf16[4,360,640]{2,1,0:T(8,128)(2,1)S(1)}, bf16[4,360,640]{2,1,0:T(8,128)(2,1)}, u32[]{:S(2)}) copy-start(bf16[4,360,640]{2,1,0:T(8,128)(2,1)} %get-tuple-element.11) | copy-start | bytes 5529604
  120.3 1.2 %copy-start.2 = (f32[80,640]{1,0:T(8,128)S(1)}, f32[80,640]{1,0:T(8,128)}, u32[]{:S(2)}) copy-start(f32[80,640]{1,0:T(8,128)} %get-tuple-element.12) | copy-start | bytes 614404
